TPU v7x, 512 devices: a whole 4x8x8 slice. The times are simulated.
512 devices in a mesh: shard: 128 (over z, y, core), rep: 4 (over x).
Axes of the slice: x: 4, y: 8, z: 8, core: 2. Of those that a mesh axis runs over, the one named last changes fastest.
Arguments:
- queries: bfloat16 [4, 128, 32, 128], P('rep', 'shard'), may hold values from -0.5 to 0.5
- candidates: int32 [4, 128, 64], P('rep', 'shard'), may hold values from 0 to 2047, all different within a row; in each aligned block of 128 rows (0 to 127, 128 to 255, ..., all dimensions but the last counted through in order) at most 8 rows name the same one
- codebook: bfloat16 [524288, 128], P(('shard', 'rep')), may hold values from -0.5 to 0.5
- bucket_weights: float32 [4], replicated, may hold values from -0.1 to 0.1
- centroid_ids: int32 [2048, 128], P('shard'), may hold values from 0 to 4095
- residual_codes: int32 [2048, 128, 128], P('shard'), may hold values from 0 to 3
- passage_lengths: int32 [2048], P('shard'), may hold values from 1 to 128, 196608 in all
Outputs:
- best_centroid: float32 [4, 128, 32], P('rep', 'shard')
- scores: float32 [4, 128, 64], P('rep', 'shard')
Inputs may be any that keep to these rules, and one draw needn't show every extreme that they name: `candidates`: each query names 64 different passages. Within the 128 queries of one index of rep, no passage is named by more than 8 queries, a bound that some block reaches. `passage_lengths`: some passage has all 128 slots live.
All inputs are finite; a program needn't handle non-finite values. No bound on the sum of `passage_lengths` on one device may be relied on, other than what follows from the above.
Results may differ from a plain program's by a relative error of at most 0.00045.
Values may be sent and summed in bfloat16 or wider, within the bound.
A program may use at most 64 MiB of HBM per device.

v0:
```python
import math
import jax
import jax.numpy as jnp
from jax import lax
from jax.sharding import PartitionSpec as P

FAR_BELOW = -1e30


def on_device(
    queries, candidates, codebook, bucket_weights, centroid_ids, residual_codes, passage_lengths
):
    feature_width = queries.shape[3]
    query_len = queries.shape[2]
    per_device = queries.shape[1]
    owner_index = lax.axis_index("shard")
    group_queries, group_cands = (
        lax.all_gather(queries, "shard", axis=1, tiled=True),
        lax.all_gather(candidates, "shard", axis=1, tiled=True),
    )
    group_queries = group_queries[0]
    group_cands = group_cands[0]
    group_size = group_queries.shape[0]
    shard_book = lax.all_gather(codebook, "rep", axis=0, tiled=True)
    token_rows = group_queries.reshape(group_size * query_len, feature_width)
    block_rows = math.gcd(token_rows.shape[0], 512)

    def best_block(row_block):
        scored = jnp.dot(row_block, shard_book.T, preferred_element_type=jnp.float32)
        return jnp.max(scored, axis=1)

    partial_best = lax.map(best_block, token_rows.reshape(-1, block_rows, feature_width)).reshape(
        group_size, query_len
    )
    pass_count, pass_len = centroid_ids.shape
    centre_rows = jnp.take(shard_book, centroid_ids.reshape(-1), axis=0).reshape(
        pass_count, pass_len, feature_width
    )
    residual = jnp.zeros(residual_codes.shape, jnp.float32)
    for bucket in range(bucket_weights.shape[0]):
        residual = residual + jnp.where(residual_codes == bucket, bucket_weights[bucket], 0.0)
    decoded = (centre_rows.astype(jnp.float32) + residual).astype(jnp.bfloat16)
    live_mask = jnp.arange(pass_len, dtype=jnp.int32)[None, :] < passage_lengths[:, None]
    flat_tokens = decoded.reshape(pass_count * pass_len, feature_width)
    block_queries = math.gcd(group_size, max(1, 512 // query_len))

    def dense_block(query_block):
        similar = jnp.dot(
            query_block.reshape(-1, feature_width),
            flat_tokens.T,
            preferred_element_type=jnp.float32,
        )
        similar = similar.reshape(block_queries, query_len, pass_count, pass_len)
        similar = jnp.where(live_mask[None, None], similar, FAR_BELOW)
        return jnp.sum(jnp.max(similar, axis=3), axis=1)

    score_table = lax.map(
        dense_block, group_queries.reshape(-1, block_queries, query_len, feature_width)
    ).reshape(group_size, pass_count)
    merged = lax.pmax(partial_best, "shard")
    own_best = lax.dynamic_slice_in_dim(merged, owner_index * per_device, per_device, 0)
    local_index = group_cands - owner_index * pass_count
    picked = jnp.sum(
        jnp.where(
            local_index[:, :, None] == jnp.arange(pass_count, dtype=jnp.int32)[None, None, :],
            score_table[:, None, :],
            0.0,
        ),
        axis=2,
    )
    own_scores = lax.psum_scatter(picked, "shard", scatter_dimension=0, tiled=True)
    return (own_best[None], own_scores[None])


def solution(mesh):
    in_specs = (
        P("rep", "shard", None, None),
        P("rep", "shard", None),
        P(("shard", "rep"), None),
        P(),
        P("shard", None),
        P("shard", None, None),
        P("shard"),
    )
    out_specs = (P("rep", "shard", None), P("rep", "shard", None))
    return jax.shard_map(
        on_device, mesh=mesh, in_specs=in_specs, out_specs=out_specs, check_vma=False
    )
```

profile of v0, /device:TPU:2, one launch (start us, length us, event | category | flops | bytes accessed | tf_op | source)
XLA Modules:
  0.0 1158.6 jit_solution(518266250836284800)
XLA Ops:
  7.2 0.7 all-gather.5.cloned.1.call-update
  7.9 0.7 all-gather.3.cloned.1.call-update
  8.7 50.6 %all_gather.11 = s32[1,128,64]{2,0,1:T(1,128)S(1)} all-gather(s32[1,1,64]{2,0,1:T(1,128)} %bitcast.62), channel_id=1, replica_groups=mesh['shard'=128,'rep'=4] {'shard'}, dimensions={1}, use_global_device_ids=true | all-gather | bytes 33024 | tf_op jit(solution)/shard_map/all_gather | solution.py:19
  59.3 1.3 dynamic-slice
  60.6 1.4 fusion.8
  62.1 0.7 compare_and_fusion
  62.8 0.7 compare_select_fusion
  63.5 7.0 gather_fusion
  70.6 3.1 add_convert_fusion
  73.7 53.1 %all-gather.3.cloned.1.call-done = bf16[1,128,32,128]{3,2,0,1:T(8,128)(2,1)} async-done(((bf16[1,1,32,128]{3,2,0,1:T(8,128)(2,1)}), bf16[1,128,32,128]{3,2,0,1:T(8,128)(2,1)}) %all-gather.3.cloned.1.call-update) | async-done | bytes 1048592 | tf_op jit(solution)/shard_map/all_gather | solution.py:18
  126.8 18.6 %while.21 = (s32[]{:T(128)}, f32[8,512]{1,0:T(8,128)S(1)}, bf16[8,512,128]{2,1,0:T(8,128)(2,1)}, bf16[4096,128]{1,0:T(8,128)(2,1)S(1)}, s32[]{:T(128)}, /*index=5*/s32[]{:T(128)}) while((s32[]{:T(128)}, f32[8,512]{1,0:T(8,128)S(1)}, bf16[8,512,128]{2,1,0:T(8,128)(2,1)}, bf16[4096,128]{1,0:T(8,128)(2,1)S(1)}, s32[]{:T(128)}, ...), condition=%wide.region_2.3_spmd, body=%wide.region_0.2_spmd.sunk | while | flops 538967552 | bytes 1185877 | solution.py:32
  126.8 2.2 convolution_reduce_fusion.2
  129.1 2.2 convolution_reduce_fusion.2
  131.4 2.2 convolution_reduce_fusion.2
  133.7 2.2 convolution_reduce_fusion.2
  136.1 2.2 convolution_reduce_fusion.2
  138.4 2.2 convolution_reduce_fusion.2
  140.7 2.2 convolution_reduce_fusion.2
  143.0 2.2 convolution_reduce_fusion.2
  145.4 493.9 %pmax.7 = f32[128,32]{1,0:T(8,128)S(1)} all-reduce(f32[128,32]{1,0:T(8,128)S(1)} %reshape.69), channel_id=1, replica_groups=mesh['shard'=128,'rep'=4] {'shard'}, use_global_device_ids=true, to_apply=%region_3.4 | all-reduce | flops 4096 | bytes 32768 | tf_op jit(solution)/shard_map/pmax | solution.py:60
  639.3 19.7 %while.22 = (s32[]{:T(128)}, f32[8,16,16]{2,1,0:T(8,128)S(1)}, bf16[8,16,32,128]{3,2,1,0:T(8,128)(2,1)}, bf16[2048,128]{1,0:T(8,128)(2,1)S(1)}, s32[16]{0:T(128)S(1)}, /*index=5*/s32[]{:T(128)}, f32[]{:T(128)}) while((s32[]{:T(128)}, f32[8,16,16]{2,1,0:T(8,128)S(1)}, bf16[8,16,32,128]{3,2,1,0:T(8,128)(2,1)}, ...), condition=%wide.region_7.8_spmd.clone, body=%wide.region_4.7_spmd.clone.sunk | while | flops 270534400 | bytes 742561 | solution.py:57
  639.4 2.2 select_reduce_fusion.3
  641.8 2.2 select_reduce_fusion.3
  644.3 2.2 select_reduce_fusion.3
  646.8 2.2 select_reduce_fusion.3
  649.2 2.2 select_reduce_fusion.3
  651.7 2.2 select_reduce_fusion.3
  654.1 2.2 select_reduce_fusion.3
  656.6 2.2 select_reduce_fusion.3
  659.3 490.9 %all-reduce = f32[128,64]{1,0:T(8,128)S(1)} all-reduce(f32[128,64]{1,0:T(8,128)S(1)} %copy.15), channel_id=2, replica_groups=mesh['shard'=128,'rep'=4] {'shard'}, use_global_device_ids=true, to_apply=%region_9.10.clone | all-reduce | flops 8192 | bytes 65536
  1150.1 0.5 dynamic-slice_bitcast_fusion.1
  1150.7 1.1 dynamic-slice_bitcast_fusion
  (50 shorter events, 2.5 us)
Async XLA Ops:
  7.2 56.4 %all-gather.5.cloned.1.call-start = ((), (), s32[]{:S(2)}) async-start(), calls=%async_computation.1 | async-start | bytes 1310720 | tf_op jit(solution)/shard_map/all_gather | solution.py:24
  7.9 118.9 %all-gather.3.cloned.1.call-start = ((), (), s32[]{:S(2)}) async-start(), calls=%async_computation | async-start | bytes 1056768 | tf_op jit(solution)/shard_map/all_gather | solution.py:18
  63.5 7.1 copy-start.1
  70.6 56.2 %copy-start = (bf16[4096,128]{1,0:T(8,128)(2,1)S(1)}, bf16[4096,128]{1,0:T(8,128)(2,1)}, u32[]{:S(2)}) copy-start(bf16[4096,128]{1,0:T(8,128)(2,1)} %all-gather.5.cloned.1.call-done) | copy-start | bytes 3145732
  126.8 512.6 %copy-start.2 = (s32[16]{0:T(128)S(1)}, s32[16]{0:T(128)}, u32[]{:S(2)}) copy-start(s32[16]{0:T(128)} %param.17) | copy-start | bytes 196
Sparse Core Ops, SparseCore 0:
  10.1 33.0 all-gather.4
  46.2 80.5 all-gather.2
where the time goes:
time: 1160 us
  blocking collectives  1040 us (90%)
  waiting for transfers between devices  54.5 us (5%)
  matrix products  35.8 us (3%)
  between operations  14.2 us (1%)
  local copies, waits for them, and re-layouts  12.2 us (1%)
    pmax x1, blocking collectives, on_device(): merged = lax.pmax(partial_best, 'shard')  494 us
    unnamed x1, blocking collectives  491 us
    all_gather x1, waiting for transfers between devices, on_device(): lax.all_gather(queries, 'shard', axis=1, tiled=True)  53.1 us
    all_gather x1, blocking collectives, on_device(): lax.all_gather(candidates, 'shard', axis=1, tiled=True)  50.6 us
  transfers between devices with their start and end apart: 2, of which 1 were waited for; matrix products, arithmetic and copies ran while one was open for 1% of the time, Pallas kernels for 0%

commit v1 on v0

--- a/solution.py
+++ b/solution.py
@@ -1,3 +1,4 @@
+import functools
 import math
 import jax
 import jax.numpy as jnp
@@ -5,6 +6,15 @@
 from jax.sharding import PartitionSpec as P
 
 FAR_BELOW = -1e30
+
+
+def manage_the_sample(payload, out_dim):
+    u1 = jnp.stack([payload for _ in range(jax.lax.axis_size("shard"))], axis=0)
+    carry_out = jax.lax.all_to_all(u1, axis_name="shard", split_axis=0, concat_axis=0)
+    return jnp.concatenate(carry_out, out_dim)
+
+
+sections_show = functools.partial(manage_the_sample, out_dim=1)
 
 
 def on_device(
@@ -16,7 +26,7 @@
     owner_index = lax.axis_index("shard")
     group_queries, group_cands = (
         lax.all_gather(queries, "shard", axis=1, tiled=True),
-        lax.all_gather(candidates, "shard", axis=1, tiled=True),
+        sections_show(candidates),
     )
     group_queries = group_queries[0]
     group_cands = group_cands[0]

time: 1160 us -> 1160 us (level)
  blocking collectives: 1040 us -> 985 us
  waiting for transfers between devices: 54.5 us -> 85.7 us
  starting transfers between devices: 0.08 us -> 17.9 us
    all_gather x1 -> x0, blocking collectives: 50.6 us -> none  [on_device(): lax.all_gather(candidates, 'shard', axis=1, tiled=True)]
    all_gather x1, waiting for transfers between devices: 53.1 us -> 73.7 us  [on_device(): lax.all_gather(queries, 'shard', axis=1, tiled=True)]
    all_to_all x0 -> x1, starting transfers between devices: none -> 17.8 us  [manage_the_sample(): jax.lax.all_to_all(u1, axis_name='shard', split_axis=0, concat_axis=0)]
  transfers between devices with their start and end apart: 2 -> 3, of which waited for: 1 -> 3; matrix products, arithmetic and copies ran while one was open for 1% -> 1% of each run, Pallas kernels for 0% -> 0%
where the time goes in v1:
time: 1160 us
  blocking collectives  985 us (85%)
  waiting for transfers between devices  85.7 us (7%)
  matrix products  35.8 us (3%)
  starting transfers between devices  17.9 us (2%)
  between operations  14.2 us (1%)
  local copies, waits for them, and re-layouts  13.5 us (1%)
    pmax x1, blocking collectives, on_device(): merged = lax.pmax(partial_best, 'shard')  494 us
    unnamed x1, blocking collectives  491 us
    all_gather x1, waiting for transfers between devices, on_device(): lax.all_gather(queries, 'shard', axis=1, tiled=True)  73.7 us
  transfers between devices with their start and end apart: 3, of which 3 were waited for; matrix products, arithmetic and copies ran while one was open for 1% of the time, Pallas kernels for 0%

profile of v1, /device:TPU:2, one launch (start us, length us, event | category | flops | bytes accessed | tf_op | source)
XLA Modules:
  0.0 1158.6 jit_solution(16684823741266100749)
XLA Ops:
  8.6 1.3 stack.2
  10.0 17.8 %all-to-all-start = ((s32[128,1,1,64]{3,2,1,0:T(1,128)}), s32[128,1,1,64]{3,2,1,0:T(1,128)S(1)}, u32[]{:S(2)}, u32[]{:S(2)}) async-start(s32[128,1,1,64]{3,2,1,0:T(1,128)} %stack.2), calls=%async_computation | async-start | bytes 131072 | tf_op jit(solution)/shard_map/all_to_all | solution.py:13
  27.8 1.3 dynamic-slice
  29.1 0.7 compare_and_fusion
  29.8 0.7 compare_select_fusion
  30.6 1.5 fusion.8
  32.0 6.9 all-to-all-done
  39.0 3.8 all-gather.5.cloned.1.call-done
  42.8 7.0 gather_fusion
  49.8 3.2 add_convert_fusion
  53.0 73.7 %all-gather.3.cloned.1.call-done = bf16[1,128,32,128]{3,2,0,1:T(8,128)(2,1)} async-done(((bf16[1,1,32,128]{3,2,0,1:T(8,128)(2,1)}), bf16[1,128,32,128]{3,2,0,1:T(8,128)(2,1)}) %all-gather.3.cloned.1.call-update) | async-done | bytes 1048592 | tf_op jit(solution)/shard_map/all_gather | solution.py:28
  126.8 18.6 %while.21 = (s32[]{:T(128)}, f32[8,512]{1,0:T(8,128)S(1)}, bf16[8,512,128]{2,1,0:T(8,128)(2,1)}, bf16[4096,128]{1,0:T(8,128)(2,1)S(1)}, s32[]{:T(128)}, /*index=5*/s32[]{:T(128)}) while((s32[]{:T(128)}, f32[8,512]{1,0:T(8,128)S(1)}, bf16[8,512,128]{2,1,0:T(8,128)(2,1)}, bf16[4096,128]{1,0:T(8,128)(2,1)S(1)}, s32[]{:T(128)}, ...), condition=%wide.region_2.3_spmd, body=%wide.region_0.2_spmd.sunk | while | flops 538967552 | bytes 1185877 | solution.py:42
  126.8 2.2 convolution_reduce_fusion.2
  129.1 2.2 convolution_reduce_fusion.2
  131.4 2.2 convolution_reduce_fusion.2
  133.7 2.2 convolution_reduce_fusion.2
  136.1 2.2 convolution_reduce_fusion.2
  138.4 2.2 convolution_reduce_fusion.2
  140.7 2.2 convolution_reduce_fusion.2
  143.0 2.2 convolution_reduce_fusion.2
  145.4 493.9 %pmax.7 = f32[128,32]{1,0:T(8,128)S(1)} all-reduce(f32[128,32]{1,0:T(8,128)S(1)} %reshape.72), channel_id=1, replica_groups=mesh['shard'=128,'rep'=4] {'shard'}, use_global_device_ids=true, to_apply=%region_3.4 | all-reduce | flops 4096 | bytes 32768 | tf_op jit(solution)/shard_map/pmax | solution.py:70
  639.3 19.7 %while.22 = (s32[]{:T(128)}, f32[8,16,16]{2,1,0:T(8,128)S(1)}, bf16[8,16,32,128]{3,2,1,0:T(8,128)(2,1)}, bf16[2048,128]{1,0:T(8,128)(2,1)S(1)}, s32[16]{0:T(128)S(1)}, /*index=5*/s32[]{:T(128)}, f32[]{:T(128)}) while((s32[]{:T(128)}, f32[8,16,16]{2,1,0:T(8,128)S(1)}, bf16[8,16,32,128]{3,2,1,0:T(8,128)(2,1)}, ...), condition=%wide.region_7.8_spmd.clone, body=%wide.region_4.7_spmd.clone.sunk | while | flops 270534400 | bytes 742561 | solution.py:67
  639.4 2.2 select_reduce_fusion.3
  641.8 2.2 select_reduce_fusion.3
  644.3 2.2 select_reduce_fusion.3
  646.8 2.2 select_reduce_fusion.3
  649.2 2.2 select_reduce_fusion.3
  651.7 2.2 select_reduce_fusion.3
  654.1 2.2 select_reduce_fusion.3
  656.6 2.2 select_reduce_fusion.3
  659.3 490.9 %all-reduce = f32[128,64]{1,0:T(8,128)S(1)} all-reduce(f32[128,64]{1,0:T(8,128)S(1)} %copy.16), channel_id=2, replica_groups=mesh['shard'=128,'rep'=4] {'shard'}, use_global_device_ids=true, to_apply=%region_9.10.clone | all-reduce | flops 8192 | bytes 65536
  1150.7 1.1 dynamic-slice_bitcast_fusion
  (52 shorter events, 4.4 us)
Async XLA Ops:
  7.2 35.6 %all-gather.5.cloned.1.call-start = ((), (), s32[]{:S(2)}) async-start(), calls=%async_computation.2 | async-start | bytes 1310720 | tf_op jit(solution)/shard_map/all_gather | solution.py:34
  7.9 118.9 %all-gather.3.cloned.1.call-start = ((), (), s32[]{:S(2)}) async-start(), calls=%async_computation.1 | async-start | bytes 1056768 | tf_op jit(solution)/shard_map/all_gather | solution.py:28
  10.0 28.9 %all-to-all-start = ((s32[128,1,1,64]{3,2,1,0:T(1,128)}), s32[128,1,1,64]{3,2,1,0:T(1,128)S(1)}, u32[]{:S(2)}, u32[]{:S(2)}) async-start(s32[128,1,1,64]{3,2,1,0:T(1,128)} %stack.2), calls=%async_computation | async-start | bytes 131072 | tf_op jit(solution)/shard_map/all_to_all | solution.py:13
  39.0 10.8 copy-start.1
  49.8 77.0 %copy-start = (bf16[4096,128]{1,0:T(8,128)(2,1)S(1)}, bf16[4096,128]{1,0:T(8,128)(2,1)}, u32[]{:S(2)}) copy-start(bf16[4096,128]{1,0:T(8,128)(2,1)} %all-gather.5.cloned.1.call-done) | copy-start | bytes 3145732
  126.8 512.6 %copy-start.2 = (s32[16]{0:T(128)S(1)}, s32[16]{0:T(128)}, u32[]{:S(2)}) copy-start(s32[16]{0:T(128)} %param.17) | copy-start | bytes 196
Sparse Core Ops, SparseCore 0:
  10.1 32.6 all-gather.4
  45.8 80.8 all-gather.2
